TPU v7x, 32 devices: a whole 2x2x4 slice. The times are simulated.
32 devices in a mesh: segment: 2 (over x), dp: 4 (over z), mp: 4 (over y, core).
Axes of the slice: x: 2, y: 2, z: 4, core: 2. Of those that a mesh axis runs over, the one named last changes fastest.
Arguments:
- images: bfloat16 [8, 128, 3840], P(('segment', 'dp')), may hold values from -6 to 6
- ln_gain: float32 [1280], replicated, may hold values from 0.1 to 1.9
- projector: bfloat16 [3840, 8192], P(None, 'mp'), may hold values from -0.09375 to 0.09375
- tile_counts: int32 [8], P(('segment', 'dp')), may hold values from 1 to 4
- assign: int32 [8], P(('segment', 'dp')), may hold values from 0 to 7, as said below
- text: bfloat16 [8, 64, 8192], P('dp', None, 'mp'), may hold values from -6 to 6
- text_start: int32 [8], P('dp'), may hold values from 0 to 32
- w_query: bfloat16 [2, 8192, 4096], P('segment', 'mp'), may hold values from -0.0625 to 0.0625
- w_key: bfloat16 [2, 8192, 512], P('segment', 'mp'), may hold values from -0.0625 to 0.0625
- w_value: bfloat16 [2, 8192, 512], P('segment', 'mp'), may hold values from -0.0625 to 0.0625
- w_out: bfloat16 [2, 4096, 8192], P('segment', None, 'mp'), may hold values from -0.09375 to 0.09375
- gates: float32 [2], P('segment'), may hold values from -1.5 to 1.5
- grad_out: bfloat16 [8, 64, 8192], P('dp', None, 'mp'), may hold values from -6 to 6
Outputs:
- phase_grads: bfloat16 [2, 8, 64, 8192], P('segment', 'dp', None, 'mp')
- feature_grads: bfloat16 [8, 128, 3840], P(('segment', 'dp'))
Inputs may be any that keep to these rules, and one draw needn't show every extreme that they name: assign is a permutation of the 8 sequences; sequence j belongs to index j // 2 of dp, image e is encoded on index e // 4 of segment and index e % 4 of dp, and the images of one index of segment belong to sequences of 4 different indices of dp.
All inputs are finite; a program needn't handle non-finite values.
Results may differ from a plain program's by a relative error of at most 0.035.
Values may be sent and summed in bfloat16 or wider, within the bound.
A program may use at most 192 MiB of HBM per device.

v0:
```python
import jax
import jax.numpy as jnp
from jax import lax
from jax.sharding import PartitionSpec as P

HD = 128
PATCH = 32


def from_behind(value, axis, steps):
    count = lax.axis_size(axis)
    leading, last = (max(0, -steps), min(count, count - steps))
    return lax.ppermute(value, axis, [(source, source + steps) for source in range(leading, last)])


def attend(query, keys, values, key_mask):
    length = query.shape[0]
    local_groups = keys.shape[1]
    group_size = query.shape[1] // (local_groups * HD)
    query_heads = query.reshape(length, local_groups, group_size, HD)
    scores = jnp.einsum(
        "tkgd,rkd->kgtr", query_heads, keys, preferred_element_type=jnp.float32
    ) * HD ** (-0.5)
    scores = jnp.where(key_mask[None, None, None, :], scores, -1e30)
    row_top = jnp.max(scores, axis=-1, keepdims=True)
    raised = jnp.exp(scores - row_top)
    prob_full = raised / jnp.sum(raised, axis=-1, keepdims=True)
    prob_half = prob_full.astype(jnp.bfloat16)
    mixed = jnp.einsum("kgtr,rkd->tkgd", prob_half, values, preferred_element_type=jnp.float32)
    return (
        prob_full,
        prob_half,
        mixed.astype(jnp.bfloat16).reshape(length, local_groups * group_size * HD),
    )


def pick_row(array, batch_slot):
    return lax.dynamic_index_in_dim(array, batch_slot, 0, keepdims=False)


def local(
    images,
    ln_gain,
    projector,
    tile_counts,
    assign,
    text,
    text_start,
    w_query,
    w_key,
    w_value,
    w_out,
    gates,
    grad_out,
):
    segments = lax.axis_size("segment")
    groups = lax.axis_size("dp")
    segment_id = lax.axis_index("segment")
    group_id = lax.axis_index("dp")
    micro_count = text.shape[0]
    length = text.shape[1]
    feat_width = text.shape[2]
    rows_img = images.shape[1]
    last_width = ln_gain.shape[0]
    local_heads = w_query.shape[2] // HD // lax.axis_size("mp")
    gate_value = jnp.tanh(gates[0])
    query_weight = w_query[0]
    out_weight = w_out[0]
    key_weight = w_key[0]
    value_weight = w_value[0]
    last_cols = images[0][:, :last_width].astype(jnp.float32)
    center = last_cols - jnp.mean(last_cols, axis=-1, keepdims=True)
    variance = jnp.mean(center * center, axis=-1, keepdims=True)
    inv_std = lax.rsqrt(variance + 1e-05)
    normed = center * inv_std
    tile_in = jnp.concatenate(
        [(normed * ln_gain).astype(jnp.bfloat16), images[0][:, last_width:]], axis=1
    )
    features = jnp.dot(tile_in, projector, preferred_element_type=jnp.float32).astype(jnp.bfloat16)
    block_rows = rows_img // groups
    pieces = features.reshape(groups, block_rows, feat_width)
    spread_assign = jnp.broadcast_to(assign, (groups,))
    spread_counts = jnp.broadcast_to(tile_counts, (groups,))
    landed, source_assign, source_counts = (
        lax.all_to_all(pieces, "dp", split_axis=0, concat_axis=0, tiled=True),
        lax.all_to_all(spread_assign, "dp", split_axis=0, concat_axis=0, tiled=True),
        lax.all_to_all(spread_counts, "dp", split_axis=0, concat_axis=0, tiled=True),
    )
    routing = source_assign[None, :] // micro_count == jnp.arange(groups, dtype=jnp.int32)[:, None]
    forwarded = jnp.einsum(
        "tg,grc->trc", routing.astype(jnp.bfloat16), landed, preferred_element_type=jnp.float32
    ).astype(jnp.bfloat16)
    forward_assign = jnp.sum(jnp.where(routing, source_assign[None, :], 0), axis=1)
    forward_counts = jnp.sum(jnp.where(routing, source_counts[None, :], 0), axis=1)
    arrived, arrived_assign, arrived_counts = (
        lax.all_to_all(forwarded, "dp", split_axis=0, concat_axis=0, tiled=True),
        lax.all_to_all(forward_assign, "dp", split_axis=0, concat_axis=0, tiled=True),
        lax.all_to_all(forward_counts, "dp", split_axis=0, concat_axis=0, tiled=True),
    )
    own_feat = arrived.reshape(rows_img, feat_width)
    own_assign = arrived_assign[0]
    own_count = arrived_counts[0]
    column_feats, column_assign, column_counts = (
        lax.all_gather(own_feat[None], "segment", axis=0, tiled=True),
        lax.all_gather(own_assign[None], "segment", axis=0, tiled=True),
        lax.all_gather(own_count[None], "segment", axis=0, tiled=True),
    )
    seq_ids = group_id * micro_count + jnp.arange(micro_count, dtype=jnp.int32)
    chosen = column_assign[None, :] == seq_ids[:, None]
    chosen_feats = jnp.einsum(
        "ik,krc->irc", chosen.astype(jnp.bfloat16), column_feats, preferred_element_type=jnp.float32
    ).astype(jnp.bfloat16)
    counts = jnp.sum(jnp.where(chosen, column_counts[None, :], 0), axis=1)
    anchor = jnp.sum(jnp.where(chosen, jnp.arange(segments, dtype=jnp.int32)[None, :], 0), axis=1)
    key_part = jnp.einsum(
        "irc,cf->irf", chosen_feats, key_weight, preferred_element_type=jnp.float32
    )
    value_part = jnp.einsum(
        "irc,cf->irf", chosen_feats, value_weight, preferred_element_type=jnp.float32
    )
    keys_here, values_here = (
        lax.psum_scatter(
            key_part.astype(jnp.bfloat16), "mp", scatter_dimension=2, tiled=True
        ).astype(jnp.float32),
        lax.psum_scatter(
            value_part.astype(jnp.bfloat16), "mp", scatter_dimension=2, tiled=True
        ).astype(jnp.float32),
    )
    local_groups = keys_here.shape[2] // HD
    group_size = local_heads // local_groups
    keys_local = keys_here.astype(jnp.bfloat16).reshape(micro_count, rows_img, local_groups, HD)
    values_local = values_here.astype(jnp.bfloat16).reshape(micro_count, rows_img, local_groups, HD)
    key_masks = jnp.arange(rows_img, dtype=jnp.int32)[None, :] < counts[:, None] * PATCH
    text_live = (jnp.arange(length, dtype=jnp.int32)[None, :] >= text_start[:, None]).astype(
        jnp.float32
    )
    turns = micro_count + segments - 1
    query_store = jnp.zeros((micro_count, length, local_heads * HD), jnp.bfloat16)
    received = jnp.zeros((length, feat_width), jnp.bfloat16)
    for turn_index in range(turns):
        batch_index = turn_index - segment_id
        is_valid = (batch_index >= 0) & (batch_index < micro_count)
        batch_slot = jnp.clip(batch_index, 0, micro_count - 1)
        layer_in = jnp.where(segment_id == 0, pick_row(text, batch_slot), received)
        query_part = jnp.dot(layer_in, query_weight, preferred_element_type=jnp.float32)
        query = lax.psum_scatter(
            query_part.astype(jnp.bfloat16), "mp", scatter_dimension=1, tiled=True
        )
        prob_full, prob_half, mixed = attend(
            query,
            pick_row(keys_local, batch_slot),
            pick_row(values_local, batch_slot),
            pick_row(key_masks, batch_slot),
        )
        projected = jnp.dot(
            lax.all_gather(mixed, "mp", axis=1, tiled=True),
            out_weight,
            preferred_element_type=jnp.float32,
        )
        live_rows = pick_row(text_live, batch_slot)[:, None]
        layer_out = (layer_in.astype(jnp.float32) + gate_value * live_rows * projected).astype(
            jnp.bfloat16
        )
        query_store = jnp.where(
            is_valid,
            lax.dynamic_update_index_in_dim(query_store, query, batch_slot, 0),
            query_store,
        )
        received = from_behind(layer_out, "segment", 1)
    grads_store = jnp.zeros((micro_count, length, feat_width), jnp.bfloat16)
    key_store = jnp.zeros((micro_count, rows_img, local_groups, HD), jnp.float32)
    value_store = jnp.zeros((micro_count, rows_img, local_groups, HD), jnp.float32)
    received_back = jnp.zeros((length, feat_width), jnp.bfloat16)
    for turn_index in range(turns):
        batch_index = turn_index - (segments - 1 - segment_id)
        is_valid = (batch_index >= 0) & (batch_index < micro_count)
        batch_slot = jnp.clip(batch_index, 0, micro_count - 1)
        cotangent = jnp.where(
            segment_id == segments - 1, pick_row(grad_out, batch_slot), received_back
        )
        live_rows = pick_row(text_live, batch_slot)[:, None]
        out_cot = (gate_value * live_rows * cotangent.astype(jnp.float32)).astype(jnp.bfloat16)
        mixed_part = lax.dot_general(
            out_cot, out_weight, (((1,), (1,)), ((), ())), preferred_element_type=jnp.float32
        )
        mixed_cot = lax.psum_scatter(
            mixed_part.astype(jnp.bfloat16), "mp", scatter_dimension=1, tiled=True
        )
        query = pick_row(query_store, batch_slot)
        keys_now = pick_row(keys_local, batch_slot)
        values_now = pick_row(values_local, batch_slot)
        prob_full, prob_half, mixed = attend(
            query, keys_now, values_now, pick_row(key_masks, batch_slot)
        )
        query_heads = query.reshape(length, local_groups, group_size, HD)
        mixed_heads = mixed_cot.reshape(length, local_groups, group_size, HD)
        prob_cot = jnp.einsum(
            "tkgd,rkd->kgtr", mixed_heads, values_now, preferred_element_type=jnp.float32
        )
        score_cot = (
            prob_full
            * (prob_cot - jnp.sum(prob_cot * prob_full, axis=-1, keepdims=True))
            * HD ** (-0.5)
        ).astype(jnp.bfloat16)
        query_cot = (
            jnp.einsum("kgtr,rkd->tkgd", score_cot, keys_now, preferred_element_type=jnp.float32)
            .astype(jnp.bfloat16)
            .reshape(length, local_heads * HD)
        )
        key_cot = jnp.einsum(
            "kgtr,tkgd->rkd", score_cot, query_heads, preferred_element_type=jnp.float32
        )
        value_cot = jnp.einsum(
            "kgtr,tkgd->rkd", prob_half, mixed_heads, preferred_element_type=jnp.float32
        )
        query_back = lax.dot_general(
            lax.all_gather(query_cot, "mp", axis=1, tiled=True),
            query_weight,
            (((1,), (1,)), ((), ())),
            preferred_element_type=jnp.float32,
        )
        layer_grad = (cotangent.astype(jnp.float32) + query_back).astype(jnp.bfloat16)
        grads_store = jnp.where(
            is_valid,
            lax.dynamic_update_index_in_dim(grads_store, layer_grad, batch_slot, 0),
            grads_store,
        )
        key_store = jnp.where(
            is_valid, lax.dynamic_update_index_in_dim(key_store, key_cot, batch_slot, 0), key_store
        )
        value_store = jnp.where(
            is_valid,
            lax.dynamic_update_index_in_dim(value_store, value_cot, batch_slot, 0),
            value_store,
        )
        received_back = from_behind(layer_grad, "segment", -1)
    key_rounded = key_store.astype(jnp.bfloat16).reshape(micro_count, rows_img, local_groups * HD)
    value_rounded = value_store.astype(jnp.bfloat16).reshape(
        micro_count, rows_img, local_groups * HD
    )
    pieces = (
        lax.all_gather(key_rounded, "mp", axis=2, tiled=True),
        lax.all_gather(value_rounded, "mp", axis=2, tiled=True),
    )
    running = lax.dot_general(
        pieces[0], key_weight, (((2,), (1,)), ((), ())), preferred_element_type=jnp.float32
    )
    feature_cot = running + lax.dot_general(
        pieces[1], value_weight, (((2,), (1,)), ((), ())), preferred_element_type=jnp.float32
    )
    placement = (anchor[:, None] == jnp.arange(segments, dtype=jnp.int32)[None, :]).astype(
        jnp.float32
    )
    outgoing = jnp.einsum("is,irc->src", placement, feature_cot, precision=lax.Precision.HIGHEST)
    summed = lax.psum_scatter(
        outgoing.astype(jnp.bfloat16), "segment", scatter_dimension=0, tiled=True
    ).astype(jnp.float32)
    returned = summed[0].astype(jnp.bfloat16)
    back_pieces = returned.reshape(groups, block_rows, feat_width)
    gathered_back = lax.all_to_all(back_pieces, "dp", split_axis=0, concat_axis=0, tiled=True)
    reordered = jnp.einsum(
        "tg,trc->grc",
        routing.astype(jnp.bfloat16),
        gathered_back,
        preferred_element_type=jnp.float32,
    ).astype(jnp.bfloat16)
    delivered = lax.all_to_all(reordered, "dp", split_axis=0, concat_axis=0, tiled=True)
    feature_back = delivered.reshape(rows_img, feat_width)
    norm_part = lax.dot_general(
        feature_back, projector, (((1,), (1,)), ((), ())), preferred_element_type=jnp.float32
    )
    norm_cot = lax.psum(norm_part.astype(jnp.bfloat16), "mp").astype(jnp.float32)
    scaled = norm_cot[:, :last_width] * ln_gain
    last_grad = inv_std * (
        scaled
        - jnp.mean(scaled, axis=-1, keepdims=True)
        - normed * jnp.mean(scaled * normed, axis=-1, keepdims=True)
    )
    result = jnp.concatenate([last_grad, norm_cot[:, last_width:]], axis=1)
    return (grads_store[None], result.astype(jnp.bfloat16)[None])


def solution(mesh):
    return jax.shard_map(
        local,
        mesh=mesh,
        in_specs=(
            P(("segment", "dp"), None, None),
            P(),
            P(None, "mp"),
            P(("segment", "dp")),
            P(("segment", "dp")),
            P("dp", None, "mp"),
            P("dp"),
            P("segment", "mp", None),
            P("segment", "mp", None),
            P("segment", "mp", None),
            P("segment", None, "mp"),
            P("segment"),
            P("dp", None, "mp"),
        ),
        out_specs=(P("segment", "dp", None, "mp"), P(("segment", "dp"), None, None)),
        check_vma=False,
    )
```

profile of v0, /device:TPU:0, one launch (start us, length us, event | category | flops | bytes accessed | tf_op | source)
XLA Modules:
  0.0 589.0 jit_solution(7175392396104960541)
XLA Ops:
  8.6 6.3 %all-to-all-start = ((s32[4,1,1]{2,1,0:T(1,128)}), s32[4,1,1]{2,1,0:T(1,128)S(1)}, u32[]{:S(2)}, u32[]{:S(2)}) async-start(s32[4,1,1]{2,1,0:T(1,128)} %broadcast_in_dim.190), calls=%async_computation | async-start | bytes 4096 | tf_op jit(solution)/shard_map/all_to_all | solution.py:86
  19.6 8.6 %convolution_convert_fusion.5 = bf16[128,2048]{1,0:T(8,128)(2,1)} fusion(bf16[3840,2048]{1,0:T(8,128)(2,1)} %param.15, bf16[128,2560]{1,0:T(8,128)(2,1)S(1)} %slice.39, bf16[128,1280]{1,0:T(8,128)(2,1)S(1)} %fusion.141), kind=kOutput, calls=%fused_computation.34 | convolution fusion | flops 2015494144 | bytes 17235968 | tf_op jit(solution)/shard_map/dot_general | solution.py:79
  28.1 5.2 all-to-all-start.2
  33.6 13.7 %all-to-all-done.2 = bf16[4,32,2048]{2,1,0:T(8,128)(2,1)S(1)} async-done(((bf16[4,32,2048]{2,1,0:T(8,128)(2,1)}), bf16[4,32,2048]{2,1,0:T(8,128)(2,1)S(1)}, u32[]{:S(2)}, u32[]{:S(2)}) %all-to-all-start.2) | async-done | bytes 524320 | tf_op jit(solution)/shard_map/all_to_all | solution.py:85
  48.3 17.1 %all_to_all.53 = bf16[4,32,2048]{2,1,0:T(8,128)(2,1)} all-to-all(bf16[4,32,2048]{2,1,0:T(8,128)(2,1)S(1)} %copy.91), channel_id=1, replica_groups=mesh['segment'=2,'dp'=4,'mp'=4] {'dp'}, dimensions={0} | all-to-all | bytes 1048576 | tf_op jit(solution)/shard_map/all_to_all | solution.py:96
  66.6 3.2 all-to-all-start.4
  70.4 4.8 all-to-all-done.4
  76.3 7.9 %all_to_all.54 = s32[4,1,1]{2,1,0:T(1,128)S(1)} all-to-all(s32[4,1,1]{2,1,0:T(1,128)S(1)} %copy.94), channel_id=1, replica_groups=mesh['segment'=2,'dp'=4,'mp'=4] {'dp'}, dimensions={0} | all-to-all | bytes 32 | tf_op jit(solution)/shard_map/all_to_all | solution.py:98
  84.1 3.2 all-to-all-start.1
  88.0 1.3 bitcast_dynamic-update-slice_fusion.2
  89.2 3.6 all-to-all-done.1
  93.3 1.3 bitcast_dynamic-update-slice_fusion.3
  94.7 4.3 all-reduce.2
  98.9 2.5 convolution_convert_fusion.1
  102.5 2.3 fusion.93
  105.8 1.9 fusion.90
  108.7 9.7 %fusion.22 = bf16[64,4096]{1,0:T(8,128)(2,1)} fusion(bf16[1,2048,4096]{2,1,0:T(8,128)(2,1)} %param.20, bf16[2,64,2048]{2,1,0:T(8,128)(2,1)S(1)} %copy-done.4, s32[]{:T(128)S(6)} %min.20, pred[]{:T(512)S(6)} %eq.54), kind=kOutput, calls=%fused_computation.23 | convolution fusion | flops 1074135040 | bytes 17563652 | tf_op jit(solution)/shard_map/dot_general | solution.py:145
  121.5 2.7 reduce-scatter.30.cloned.1.call-done
  125.0 21.8 %reduce-scatter.28.cloned.1.call-done = bf16[128,256]{1,0:T(8,128)(2,1)} async-done(((bf16[512,256]{1,0:T(8,128)(2,1)}), bf16[128,256]{1,0:T(8,128)(2,1)}) %reduce-scatter.28.cloned.1.call-update) | async-done | bytes 65552
  147.7 1.4 constant_dynamic-slice_fusion.1
  149.3 22.1 %reduce-scatter.14.cloned.1.call-done = bf16[64,1024]{1,0:T(8,128)(2,1)} async-done(((bf16[64,4096]{1,0:T(8,128)(2,1)}), bf16[64,1024]{1,0:T(8,128)(2,1)}) %reduce-scatter.14.cloned.1.call-update) | async-done | bytes 131088 | tf_op jit(solution)/shard_map/reduce_scatter | solution.py:146
  173.4 6.8 %all_gather.33 = bf16[64,4096]{1,0:T(8,128)(2,1)S(1)} all-gather(bf16[64,1024]{1,0:T(8,128)(2,1)S(1)} %bitcast.571), channel_id=1, replica_groups=mesh['segment'=2,'dp'=4,'mp'=4] {'mp'}, dimensions={1}, use_global_device_ids=true | all-gather | bytes 655360 | tf_op jit(solution)/shard_map/all_gather | solution.py:156
  180.2 8.8 %fusion.58 = bf16[64,2048]{1,0:T(8,128)(2,1)S(1)} fusion(bf16[64,4096]{1,0:T(8,128)(2,1)S(1)} %all_gather.33, bf16[1,4096,2048]{2,1,0:T(8,128)(2,1)} %param.23, f32[64]{0:T(128)S(1)} %get-tuple-element.33, bf16[2,64,2048]{2,1,0:T(8,128)(2,1)S(1)} %copy-done.4, s32[]{:T(128)S(6)} %min.20, pred[]{:T(512)S(6)} %eq.54), kind=kOutput, calls=%fused_computation.41 | convolution fusion | flops 1074397184 | bytes 17826052 | tf_op jit(solution)/shard_map/dot_general | solution.py:155
  189.0 3.4 collective-permute-start
  192.4 6.0 %collective-permute-done = bf16[64,2048]{1,0:T(8,128)(2,1)S(1)} collective-permute-done((bf16[64,2048]{1,0:T(8,128)(2,1)S(1)}, bf16[64,2048]{1,0:T(8,128)(2,1)S(1)}, u32[]{:S(2)}, u32[]{:S(2)}) %collective-permute-start) | collective-permute-done | bytes 262176 | tf_op jit(solution)/shard_map/ppermute | solution.py:13
  198.4 9.6 %fusion.25 = bf16[64,4096]{1,0:T(8,128)(2,1)} fusion(bf16[1,2048,4096]{2,1,0:T(8,128)(2,1)} %param.20, bf16[64,2048]{1,0:T(8,128)(2,1)S(1)} %collective-permute-done, bf16[2,64,2048]{2,1,0:T(8,128)(2,1)S(1)} %copy-done.4, s32[]{:T(128)S(6)} %min.21, pred[]{:T(512)S(6)} %eq.54), kind=kOutput, calls=%fused_computation.24 | convolution fusion | flops 1074135040 | bytes 17825796 | tf_op jit(solution)/shard_map/dot_general | solution.py:145
  208.3 22.9 %reduce-scatter.16.cloned.1.call-done = bf16[64,1024]{1,0:T(8,128)(2,1)} async-done(((bf16[64,4096]{1,0:T(8,128)(2,1)}), bf16[64,1024]{1,0:T(8,128)(2,1)}) %reduce-scatter.16.cloned.1.call-update) | async-done | bytes 131088 | tf_op jit(solution)/shard_map/reduce_scatter | solution.py:146
  233.2 6.8 %all_gather.34 = bf16[64,4096]{1,0:T(8,128)(2,1)S(1)} all-gather(bf16[64,1024]{1,0:T(8,128)(2,1)S(1)} %bitcast.572), channel_id=1, replica_groups=mesh['segment'=2,'dp'=4,'mp'=4] {'mp'}, dimensions={1}, use_global_device_ids=true | all-gather | bytes 655360 | tf_op jit(solution)/shard_map/all_gather | solution.py:156
  240.0 9.5 %add_convert_fusion = bf16[64,2048]{1,0:T(8,128)(2,1)} fusion(bf16[64,4096]{1,0:T(8,128)(2,1)S(1)} %all_gather.34, bf16[1,4096,2048]{2,1,0:T(8,128)(2,1)} %param.23, f32[64]{0:T(128)S(1)} %get-tuple-element.32, bf16[64,2048]{1,0:T(8,128)(2,1)S(1)} %collective-permute-done, bf16[2,64,2048]{2,1,0:T(8,128)(2,1)S(1)} %copy-done.4, s32[]{:T(128)S(6)} %min.21, ...), kind=kOutput, calls=%fused_computation.144 | convolution fusion | flops 1074397184 | bytes 18088196 | tf_op jit(solution)/shard_map/dot_general | solution.py:155
  249.5 3.9 collective-permute-start.1
  253.4 5.9 %collective-permute-done.1 = bf16[64,2048]{1,0:T(8,128)(2,1)S(1)} collective-permute-done((bf16[64,2048]{1,0:T(8,128)(2,1)}, bf16[64,2048]{1,0:T(8,128)(2,1)S(1)}, u32[]{:S(2)}, u32[]{:S(2)}) %collective-permute-start.1) | collective-permute-done | bytes 262176 | tf_op jit(solution)/shard_map/ppermute | solution.py:13
  259.4 9.6 %fusion.28 = bf16[64,4096]{1,0:T(8,128)(2,1)} fusion(bf16[1,2048,4096]{2,1,0:T(8,128)(2,1)} %param.20, bf16[64,2048]{1,0:T(8,128)(2,1)S(1)} %collective-permute-done.1, bf16[2,64,2048]{2,1,0:T(8,128)(2,1)S(1)} %copy-done.4, s32[]{:T(128)S(6)} %min.22, pred[]{:T(512)S(6)} %eq.54), kind=kOutput, calls=%fused_computation.25 | convolution fusion | flops 1074135040 | bytes 17825796 | tf_op jit(solution)/shard_map/dot_general | solution.py:145
  269.0 11.8 %fusion.31 = bf16[64,4096]{1,0:T(8,128)(2,1)} fusion(bf16[1,4096,2048]{2,1,0:T(8,128)(2,1)} %param.23, f32[64]{0:T(128)S(1)} %get-tuple-element.31, bf16[2,64,2048]{2,1,0:T(8,128)(2,1)S(1)} %copy-done.2, s32[]{:T(128)S(6)} %min.19, pred[]{:T(512)S(6)} %eq.20), kind=kOutput, calls=%fused_computation.26 | convolution fusion | flops 1074528256 | bytes 17564164 | tf_op jit(solution)/shard_map/dot_general | solution.py:183
  283.0 9.1 %reduce-scatter.18.cloned.1.call-done = bf16[64,1024]{1,0:T(8,128)(2,1)} async-done(((bf16[64,4096]{1,0:T(8,128)(2,1)}), bf16[64,1024]{1,0:T(8,128)(2,1)}) %reduce-scatter.18.cloned.1.call-update) | async-done | bytes 131088 | tf_op jit(solution)/shard_map/reduce_scatter | solution.py:146
  295.0 22.0 %reduce-scatter.20.cloned.1.call-done = bf16[64,1024]{1,0:T(8,128)(2,1)} async-done(((bf16[64,4096]{1,0:T(8,128)(2,1)}), bf16[64,1024]{1,0:T(8,128)(2,1)}) %reduce-scatter.20.cloned.1.call-update) | async-done | bytes 131088 | tf_op jit(solution)/shard_map/reduce_scatter | solution.py:186
  319.4 6.8 %all_gather.35 = bf16[64,4096]{1,0:T(8,128)(2,1)S(1)} all-gather(bf16[64,1024]{1,0:T(8,128)(2,1)S(1)} %bitcast.573), channel_id=1, replica_groups=mesh['segment'=2,'dp'=4,'mp'=4] {'mp'}, dimensions={1}, use_global_device_ids=true | all-gather | bytes 655360 | tf_op jit(solution)/shard_map/all_gather | solution.py:217
  326.3 11.0 %bitcast_dynamic-update-slice_fusion = (bf16[2,64,2048]{2,1,0:T(8,128)(2,1)S(1)}, bf16[64,2048]{1,0:T(8,128)(2,1)S(1)}) fusion(bf16[2,64,2048]{2,1,0:T(8,128)(2,1)S(1)} %broadcast_in_dim.188, s32[]{:T(128)S(6)} %min.19, pred[]{:T(512)S(6)} %and.35, bf16[64,4096]{1,0:T(8,128)(2,1)S(1)} %all_gather.35, bf16[1,2048,4096]{2,1,0:T(8,128)(2,1)} %param.20, ...), kind=kOutput, calls=%fused_computation.155 | convolution fusion | flops 1074397184 | bytes 18087942 | tf_op jit(solution)/shard_map/dot_general | solution.py:216
  337.2 1.5 collective-permute-start.2
  338.7 9.0 %collective-permute-done.2 = bf16[64,2048]{1,0:T(8,128)(2,1)S(1)} collective-permute-done((bf16[64,2048]{1,0:T(8,128)(2,1)S(1)}, bf16[64,2048]{1,0:T(8,128)(2,1)S(1)}, u32[]{:S(2)}, u32[]{:S(2)}) %collective-permute-start.2) | collective-permute-done | bytes 262176 | tf_op jit(solution)/shard_map/ppermute | solution.py:13
  347.7 11.9 %fusion.34 = bf16[64,4096]{1,0:T(8,128)(2,1)} fusion(bf16[1,4096,2048]{2,1,0:T(8,128)(2,1)} %param.23, f32[64]{0:T(128)S(1)} %get-tuple-element.30, bf16[64,2048]{1,0:T(8,128)(2,1)S(1)} %collective-permute-done.2, bf16[2,64,2048]{2,1,0:T(8,128)(2,1)S(1)} %copy-done.2, s32[]{:T(128)S(6)} %min.23, pred[]{:T(512)S(6)} %eq.20), kind=kOutput, calls=%fused_computation.27 | convolution fusion | flops 1074528256 | bytes 17826308 | tf_op jit(solution)/shard_map/dot_general | solution.py:183
  359.7 1.5 copy.135
  361.2 1.6 copy.136
  365.7 15.2 %reduce-scatter.22.cloned.1.call-done = bf16[64,1024]{1,0:T(8,128)(2,1)} async-done(((bf16[64,4096]{1,0:T(8,128)(2,1)}), bf16[64,1024]{1,0:T(8,128)(2,1)}) %reduce-scatter.22.cloned.1.call-update) | async-done | bytes 131088 | tf_op jit(solution)/shard_map/reduce_scatter | solution.py:186
  384.1 7.4 %all_gather.36 = bf16[64,4096]{1,0:T(8,128)(2,1)} all-gather(bf16[64,1024]{1,0:T(8,128)(2,1)S(1)} %bitcast.574), channel_id=1, replica_groups=mesh['segment'=2,'dp'=4,'mp'=4] {'mp'}, dimensions={1}, use_global_device_ids=true | all-gather | bytes 655360 | tf_op jit(solution)/shard_map/all_gather | solution.py:217
  391.5 11.9 %fusion.160 = (bf16[2,64,2048]{2,1,0:T(8,128)(2,1)S(1)}, bf16[64,2048]{1,0:T(8,128)(2,1)}) fusion(bf16[2,64,2048]{2,1,0:T(8,128)(2,1)S(1)} %get-tuple-element.47, s32[]{:T(128)S(6)} %min.23, pred[]{:T(512)S(6)} %and.40, bf16[64,4096]{1,0:T(8,128)(2,1)} %all_gather.36, bf16[1,2048,4096]{2,1,0:T(8,128)(2,1)} %param.20, bf16[64,2048]{1,0:T(8,128)(2,1)} %copy-done.6, ...), kind=kOutput, calls=%fused_computation.153 | convolution fusion | flops 1074397184 | bytes 18612230 | tf_op jit(solution)/shard_map/dot_general | solution.py:216
  403.5 1.5 collective-permute-start.3
  405.0 1.6 copy.154
  409.7 4.5 collective-permute-done.3
  414.2 11.9 %fusion.37 = bf16[64,4096]{1,0:T(8,128)(2,1)} fusion(bf16[1,4096,2048]{2,1,0:T(8,128)(2,1)} %param.23, f32[64]{0:T(128)} %get-tuple-element.29, bf16[64,2048]{1,0:T(8,128)(2,1)} %collective-permute-done.3, bf16[2,64,2048]{2,1,0:T(8,128)(2,1)S(1)} %copy-done.2, s32[]{:T(128)S(6)} %min.24, pred[]{:T(512)S(6)} %eq.20), kind=kOutput, calls=%fused_computation.28 | convolution fusion | flops 1074528256 | bytes 17826052 | tf_op jit(solution)/shard_map/dot_general | solution.py:183
  432.2 15.2 %reduce-scatter.24.cloned.1.call-done = bf16[64,1024]{1,0:T(8,128)(2,1)} async-done(((bf16[64,4096]{1,0:T(8,128)(2,1)}), bf16[64,1024]{1,0:T(8,128)(2,1)}) %reduce-scatter.24.cloned.1.call-update) | async-done | bytes 131088 | tf_op jit(solution)/shard_map/reduce_scatter | solution.py:186
  450.1 5.8 all-gather.3
  457.1 5.9 all-gather.2
  463.7 2.4 convolution_add_fusion
  466.1 4.9 convolution_convert_fusion.2
  471.0 1.3 copy.118
  472.3 20.5 %reduce-scatter.26.cloned.1.call-done = bf16[1,128,2048]{2,1,0:T(8,128)(2,1)} async-done(((bf16[2,128,2048]{2,1,0:T(8,128)(2,1)}), bf16[1,128,2048]{2,1,0:T(8,128)(2,1)}) %reduce-scatter.26.cloned.1.call-update) | async-done | bytes 524304 | tf_op jit(solution)/shard_map/reduce_scatter | solution.py:255
  492.8 19.1 %all_to_all.55 = bf16[4,32,2048]{2,1,0:T(8,128)(2,1)S(1)} all-to-all(bf16[4,32,2048]{2,1,0:T(8,128)(2,1)} %bitcast.576), channel_id=1, replica_groups=mesh['segment'=2,'dp'=4,'mp'=4] {'dp'}, dimensions={0} | all-to-all | bytes 1048576 | tf_op jit(solution)/shard_map/all_to_all | solution.py:260
  513.5 3.5 all-to-all-start.7
  518.9 7.9 %all_gather.37 = bf16[64,4096]{1,0:T(8,128)(2,1)} all-gather(bf16[64,1024]{1,0:T(8,128)(2,1)S(1)} %bitcast.575), channel_id=1, replica_groups=mesh['segment'=2,'dp'=4,'mp'=4] {'mp'}, dimensions={1}, use_global_device_ids=true | all-gather | bytes 655360 | tf_op jit(solution)/shard_map/all_gather | solution.py:217
  526.8 3.8 all-to-all-done.7
  531.4 11.9 %convolution_convert_fusion = bf16[128,3840]{1,0:T(8,128)(2,1)} fusion(bf16[128,2048]{1,0:T(8,128)(2,1)} %bitcast.565, bf16[3840,2048]{1,0:T(8,128)(2,1)} %param.15), kind=kOutput, calls=%fused_computation.22 | convolution fusion | flops 2013757440 | bytes 17235968 | tf_op jit(solution)/shard_map/dot_general | solution.py:269
  543.4 12.1 %fusion.79 = bf16[1,2,64,2048]{3,2,1,0:T(8,128)(2,1)} fusion(bf16[1,2,64,2048]{3,2,1,0:T(8,128)(2,1)} %copy.244, s32[]{:T(128)S(6)} %min.24, bf16[64,4096]{1,0:T(8,128)(2,1)} %all_gather.37, bf16[1,2048,4096]{2,1,0:T(8,128)(2,1)} %param.20, bf16[2,64,2048]{2,1,0:T(8,128)(2,1)} %copy-done.3, pred[]{:T(512)S(6)} %and.41, ...), kind=kOutput, calls=%fused_computation.48 | convolution fusion | flops 1074397184 | bytes 18350086 | tf_op jit(solution)/shard_map/dot_general | solution.py:216
  555.5 21.9 %all-reduce.5.cloned.1.call-done = bf16[128,3840]{1,0:T(8,128)(2,1)} async-done(((bf16[128,3840]{1,0:T(8,128)(2,1)}), bf16[128,3840]{1,0:T(8,128)(2,1)}) %all-reduce.5.cloned.1.call-update) | async-done | bytes 983056 | tf_op jit(solution)/shard_map/psum | solution.py:272
  579.7 1.3 fusion.153
  (173 shorter events, 56.2 us)
Async XLA Ops:
  7.2 98.6 %copy-start = (bf16[1,2048,512]{2,1,0:T(8,128)(2,1)S(1)}, bf16[1,2048,512]{2,1,0:T(8,128)(2,1)}, u32[]{:S(2)}) copy-start(bf16[1,2048,512]{2,1,0:T(8,128)(2,1)} %param.21) | copy-start | bytes 6291460
  7.2 62.6 %copy-start.22 = (u32[32]{0:T(128)S(1)}, u32[32]{0:T(128)}, u32[]{:S(2)}) copy-start(u32[32]{0:T(128)} %constant.169) | copy-start | bytes 388
  8.6 19.6 %all-to-all-start = ((s32[4,1,1]{2,1,0:T(1,128)}), s32[4,1,1]{2,1,0:T(1,128)S(1)}, u32[]{:S(2)}, u32[]{:S(2)}) async-start(s32[4,1,1]{2,1,0:T(1,128)} %broadcast_in_dim.190), calls=%async_computation | async-start | bytes 4096 | tf_op jit(solution)/shard_map/all_to_all | solution.py:86
  28.1 80.6 %copy-start.4 = (bf16[2,64,2048]{2,1,0:T(8,128)(2,1)S(1)}, bf16[2,64,2048]{2,1,0:T(8,128)(2,1)}, u32[]{:S(2)}) copy-start(bf16[2,64,2048]{2,1,0:T(8,128)(2,1)} %param.18) | copy-start | bytes 1572868
  28.1 19.1 %all-to-all-start.2 = ((bf16[4,32,2048]{2,1,0:T(8,128)(2,1)}), bf16[4,32,2048]{2,1,0:T(8,128)(2,1)S(1)}, u32[]{:S(2)}, u32[]{:S(2)}) async-start(bf16[4,32,2048]{2,1,0:T(8,128)(2,1)} %bitcast.8), calls=%async_computation.2 | async-start | bytes 1048576 | tf_op jit(solution)/shard_map/all_to_all | solution.py:85
  33.4 65.6 %all-gather.6.cloned.1.call-start = ((), (), s32[]{:S(2)}) async-start(), calls=%async_computation.17 | async-start | bytes 1572864 | tf_op jit(solution)/shard_map/all_gather | solution.py:104
  33.5 84.9 %copy-start.18 = (s32[4]{0:T(128)}, s32[4]{0:T(128)S(1)}, u32[]{:S(2)}) copy-start(s32[4]{0:T(128)S(1)} %and_select_fusion) | copy-start | bytes 52
  66.6 8.7 %all-to-all-start.4 = ((s32[4,1,1]{2,1,0:T(1,128)}), s32[4,1,1]{2,1,0:T(1,128)S(1)}, u32[]{:S(2)}, u32[]{:S(2)}) async-start(s32[4,1,1]{2,1,0:T(1,128)} %broadcast_in_dim.194), calls=%async_computation.4 | async-start | bytes 4096 | tf_op jit(solution)/shard_map/all_to_all | solution.py:87
  84.1 8.7 %all-to-all-start.1 = ((s32[4,1,1]{2,1,0:T(1,128)}), s32[4,1,1]{2,1,0:T(1,128)S(1)}, u32[]{:S(2)}, u32[]{:S(2)}) async-start(s32[4,1,1]{2,1,0:T(1,128)} %copy.88), calls=%async_computation.1 | async-start | bytes 4096 | tf_op jit(solution)/shard_map/all_to_all | solution.py:97
  87.4 36.8 %reduce-scatter.30.cloned.1.call-start = ((), (), s32[]{:S(2)}) async-start(), calls=%async_computation.27 | async-start | bytes 327680
  101.5 1.0 copy-start.23
  104.8 14.7 %copy-start.21 = (s32[2]{0:T(128)S(1)}, s32[2]{0:T(128)}, u32[]{:S(2)}) copy-start(s32[2]{0:T(128)} %param.19) | copy-start | bytes 28
  105.7 41.1 %reduce-scatter.28.cloned.1.call-start = ((), (), s32[]{:S(2)}) async-start(), calls=%async_computation.26 | async-start | bytes 327680
  108.7 62.8 %reduce-scatter.14.cloned.1.call-start = ((), (), s32[]{:S(2)}) async-start(), calls=%async_computation.18 | async-start | bytes 655360 | tf_op jit(solution)/shard_map/reduce_scatter | solution.py:146
  118.5 112.8 %reduce-scatter.16.cloned.1.call-start = ((), (), s32[]{:S(2)}) async-start(), calls=%async_computation.19 | async-start | bytes 655360 | tf_op jit(solution)/shard_map/reduce_scatter | solution.py:146
  189.0 9.4 %collective-permute-start = (bf16[64,2048]{1,0:T(8,128)(2,1)S(1)}, bf16[64,2048]{1,0:T(8,128)(2,1)S(1)}, u32[]{:S(2)}, u32[]{:S(2)}) collective-permute-start(bf16[64,2048]{1,0:T(8,128)(2,1)S(1)} %fusion.58), channel_id=1, source_target_pairs={{0,16},{1,17},{2,18},{3,19},{4,20},{5,21},{6,22},{7,23},{8,24},{9,... | collective-permute-start | bytes 786440 | tf_op jit(solution)/shard_map/ppermute | solution.py:13
  208.0 84.0 %reduce-scatter.18.cloned.1.call-start = ((), (), s32[]{:S(2)}) async-start(), calls=%async_computation.20 | async-start | bytes 655360 | tf_op jit(solution)/shard_map/reduce_scatter | solution.py:146
  249.5 19.5 %copy-start.2 = (bf16[2,64,2048]{2,1,0:T(8,128)(2,1)S(1)}, bf16[2,64,2048]{2,1,0:T(8,128)(2,1)}, u32[]{:S(2)}) copy-start(bf16[2,64,2048]{2,1,0:T(8,128)(2,1)} %param.25) | copy-start | bytes 1572868
  249.5 9.9 %collective-permute-start.1 = (bf16[64,2048]{1,0:T(8,128)(2,1)}, bf16[64,2048]{1,0:T(8,128)(2,1)S(1)}, u32[]{:S(2)}, u32[]{:S(2)}) collective-permute-start(bf16[64,2048]{1,0:T(8,128)(2,1)} %add_convert_fusion), channel_id=1, source_target_pairs={{0,16},{1,17},{2,18},{3,19},{4,20},{5,21},{6,22},{7,23},{8,24},{9,... | collective-permute-start | bytes 786440 | tf_op jit(solution)/shard_map/ppermute | solution.py:13
  253.4 27.5 %copy-start.9 = (bf16[64,1024]{1,0:T(8,128)(2,1)S(1)}, bf16[64,1024]{1,0:T(8,128)(2,1)}, u32[]{:S(2)}) copy-start(bf16[64,1024]{1,0:T(8,128)(2,1)} %reduce-scatter.14.cloned.1.call-done) | copy-start | bytes 393220
  268.9 14.0 %copy-start.8 = (bf16[64,1024]{1,0:T(8,128)(2,1)S(1)}, bf16[64,1024]{1,0:T(8,128)(2,1)}, u32[]{:S(2)}) copy-start(bf16[64,1024]{1,0:T(8,128)(2,1)} %reduce-scatter.16.cloned.1.call-done) | copy-start | bytes 393220
  268.9 25.5 %copy-start.17 = (pred[128]{0:T(512)(128)(4,1)S(1)}, pred[128]{0:T(512)(128)(4,1)}, u32[]{:S(2)}) copy-start(pred[128]{0:T(512)(128)(4,1)} %get-tuple-element.38) | copy-start | bytes 388
  269.0 48.0 %reduce-scatter.20.cloned.1.call-start = ((), (), s32[]{:S(2)}) async-start(), calls=%async_computation.21 | async-start | bytes 655360 | tf_op jit(solution)/shard_map/reduce_scatter | solution.py:186
  280.8 100.1 %reduce-scatter.22.cloned.1.call-start = ((), (), s32[]{:S(2)}) async-start(), calls=%async_computation.22 | async-start | bytes 655360 | tf_op jit(solution)/shard_map/reduce_scatter | solution.py:186
  293.8 0.6 copy-start.10
  337.2 10.4 %collective-permute-start.2 = (bf16[64,2048]{1,0:T(8,128)(2,1)S(1)}, bf16[64,2048]{1,0:T(8,128)(2,1)S(1)}, u32[]{:S(2)}, u32[]{:S(2)}) collective-permute-start(bf16[64,2048]{1,0:T(8,128)(2,1)S(1)} %get-tuple-element.48), channel_id=1, source_target_pairs={{16,0},{17,1},{18,2},{19,3},{20,4},{21,5},{22,6},{23,7},{24,8},{25... | collective-permute-start | bytes 786440 | tf_op jit(solution)/shard_map/ppermute | solution.py:13
  347.7 16.0 %copy-start.6 = (bf16[64,2048]{1,0:T(8,128)(2,1)}, bf16[64,2048]{1,0:T(8,128)(2,1)S(1)}, u32[]{:S(2)}) copy-start(bf16[64,2048]{1,0:T(8,128)(2,1)S(1)} %collective-permute-done.2) | copy-start | bytes 786436
  359.6 87.8 %reduce-scatter.24.cloned.1.call-start = ((), (), s32[]{:S(2)}) async-start(), calls=%async_computation.23 | async-start | bytes 655360 | tf_op jit(solution)/shard_map/reduce_scatter | solution.py:186
  363.7 0.7 copy-start.12
  383.1 8.5 %copy-start.7 = (bf16[8,64,128]{2,1,0:T(8,128)(2,1)}, bf16[8,64,128]{2,1,0:T(8,128)(2,1)S(1)}, u32[]{:S(2)}) copy-start(bf16[8,64,128]{2,1,0:T(8,128)(2,1)S(1)} %get-tuple-element.13) | copy-start | bytes 393220
  384.1 23.8 %copy-start.11 = (bf16[8,8,8,128]{3,1,2,0:T(8,128)(2,1)S(1)}, bf16[8,8,8,128]{3,1,2,0:T(8,128)(2,1)}, u32[]{:S(2)}) copy-start(bf16[8,8,8,128]{3,1,2,0:T(8,128)(2,1)} %get-tuple-element.16) | copy-start | bytes 393220
  391.5 15.0 %copy-start.15 = (bf16[1,128,128]{1,0,2:T(2,128)(2,1)S(1)}, bf16[1,128,128]{1,0,2:T(2,128)(2,1)}, u32[]{:S(2)}) copy-start(bf16[1,128,128]{1,0,2:T(2,128)(2,1)} %get-tuple-element.24) | copy-start | bytes 98308
  391.5 15.7 %copy-start.14 = (bf16[1,128,128]{1,0,2:T(2,128)(2,1)S(1)}, bf16[1,128,128]{1,0,2:T(2,128)(2,1)}, u32[]{:S(2)}) copy-start(bf16[1,128,128]{1,0,2:T(2,128)(2,1)} %get-tuple-element.63) | copy-start | bytes 98308
  403.4 113.6 %copy-start.3 = (bf16[2,64,2048]{2,1,0:T(8,128)(2,1)}, bf16[2,64,2048]{2,1,0:T(8,128)(2,1)S(1)}, u32[]{:S(2)}) copy-start(bf16[2,64,2048]{2,1,0:T(8,128)(2,1)S(1)} %get-tuple-element.53) | copy-start | bytes 1572868
  403.5 10.8 %collective-permute-start.3 = (bf16[64,2048]{1,0:T(8,128)(2,1)}, bf16[64,2048]{1,0:T(8,128)(2,1)}, u32[]{:S(2)}, u32[]{:S(2)}) collective-permute-start(bf16[64,2048]{1,0:T(8,128)(2,1)} %get-tuple-element.54), channel_id=1, source_target_pairs={{16,0},{17,1},{18,2},{19,3},{20,4},{21,5},{22,6},{23,7},{24,8},{25... | collective-permute-start | bytes 786440 | tf_op jit(solution)/shard_map/ppermute | solution.py:13
  408.0 0.7 copy-start.13
  426.1 40.0 %copy-start.20 = (s32[2]{0:T(128)S(1)}, s32[2]{0:T(128)}, u32[]{:S(2)}) copy-start(s32[2]{0:T(128)} %get-tuple-element.4) | copy-start | bytes 28
  426.2 66.6 %reduce-scatter.26.cloned.1.call-start = ((), (), s32[]{:S(2)}) async-start(), calls=%async_computation.24 | async-start | bytes 1572864 | tf_op jit(solution)/shard_map/reduce_scatter | solution.py:255
  427.7 84.2 %copy-start.19 = (s32[4]{0:T(128)S(1)}, s32[4]{0:T(128)}, u32[]{:S(2)}) copy-start(s32[4]{0:T(128)} %copy-done.18) | copy-start | bytes 52
  513.5 17.1 %all-to-all-start.7 = ((bf16[4,32,2048]{2,1,0:T(8,128)(2,1)}), bf16[4,32,2048]{2,1,0:T(8,128)(2,1)S(1)}, u32[]{:S(2)}, u32[]{:S(2)}) async-start(bf16[4,32,2048]{2,1,0:T(8,128)(2,1)} %copy.120), calls=%async_computation.14 | async-start | bytes 1048576 | tf_op jit(solution)/shard_map/all_to_all | solution.py:267
  517.0 60.3 %all-reduce.5.cloned.1.call-start = ((), (), s32[]{:S(2)}) async-start(), calls=%async_computation.25 | async-start | bytes 1966080 | tf_op jit(solution)/shard_map/psum | solution.py:272
  530.6 0.8 copy-start.5
  531.4 46.0 %copy-start.1 = (bf16[1,128,3840]{2,1,0:T(8,128)(2,1)S(1)}, bf16[1,128,3840]{2,1,0:T(8,128)(2,1)}, u32[]{:S(2)}) copy-start(bf16[1,128,3840]{2,1,0:T(8,128)(2,1)} %param.13) | copy-start | bytes 2949124
  531.4 46.0 %copy-start.16 = (f32[1280]{0:T(1024)S(1)}, f32[1280]{0:T(1024)}, u32[]{:S(2)}) copy-start(f32[1280]{0:T(1024)} %param.14) | copy-start | bytes 15364
Sparse Core Ops, SparseCore 0:
  65.5 20.3 all-gather.5
  105.8 18.2 reduce-scatter.29
  126.8 20.0 reduce-scatter.27
  149.8 21.6 reduce-scatter.13
  208.1 23.0 reduce-scatter.15
  269.1 22.9 reduce-scatter.17
  295.3 21.6 reduce-scatter.19
  359.7 21.1 reduce-scatter.21
  426.3 21.0 reduce-scatter.23
  472.4 20.3 reduce-scatter.25
  543.5 33.8 all-reduce.4
where the time goes:
time: 599 us; the launch traced here: 589 us
  waiting for transfers between devices  225 us (38%)
  matrix products  172 us (29%)
  blocking collectives  95.5 us (16%)
  local copies, waits for them, and re-layouts  33.8 us (6%)
  starting transfers between devices  32.3 us (5%)
  between operations  17.3 us (3%)
  other arithmetic  13.4 us (2%)
    reduce_scatter x3, waiting for transfers between devices, local(): lax.psum_scatter(query_part.astype(jnp.bfloat16), 'mp', scatter_dimension...  54.1 us
    reduce_scatter x3, waiting for transfers between devices, local(): lax.psum_scatter(mixed_part.astype(jnp.bfloat16), 'mp', scatter_dimension...  52.4 us
    dot_general x3, matrix products, local(): lax.dot_general(out_cot, out_weight, (((1,), (1,)), ((), ())), preferred_...  35.6 us
    dot_general x3, matrix products, local(): lax.dot_general(lax.all_gather(query_cot, 'mp', axis=1, tiled=True), quer...  35 us
    dot_general x3, matrix products, local(): jnp.dot(layer_in, query_weight, preferred_element_type=jnp.float32)  28.9 us
    ppermute x4, waiting for transfers between devices, from_behind(): lax.ppermute(value, axis, [(source, source + steps) for source in range(l...  25.5 us
    unnamed x13, waiting for transfers between devices  24.7 us
    unnamed x82, local copies, waits for them, and re-layouts  23.4 us
  transfers between devices with their start and end apart: 20, of which 18 were waited for; matrix products, arithmetic and copies ran while one was open for 14% of the time, Pallas kernels for 0%

commit v1 on v0

v1 whole, which is shorter than its diff:
```python
import jax
import jax.numpy as jnp
from jax import lax
from jax.sharding import PartitionSpec as P

HD = 128
PATCH = 32
BF = jnp.bfloat16
F32 = jnp.float32


def swap(value, axis, bit):
    count = lax.axis_size(axis)
    return lax.ppermute(value, axis, [(i, i ^ bit) for i in range(count)])


def pick(array, index, axis=0):
    return lax.dynamic_index_in_dim(array, index, axis, keepdims=False)


def scatter_sum(parts, axis="mp"):
    index = lax.axis_index(axis)
    low, high = index % 2, index // 2
    pairs = parts.reshape((2, 2) + parts.shape[1:])
    kept = pick(pairs, low, 1) + swap(pick(pairs, 1 - low, 1).astype(BF), axis, 1).astype(F32)
    return pick(kept, high, 0) + swap(pick(kept, 1 - high, 0).astype(BF), axis, 2).astype(F32)


def scatter_columns(part):
    rows, width = part.shape
    count = lax.axis_size("mp")
    index = lax.axis_index("mp")
    low, high = index % 2, index // 2
    n = width // count

    def block(array, k):
        return lax.dynamic_slice_in_dim(array, k * n, n, 1)

    sent = jnp.concatenate([block(part, 1 - low), block(part, 3 - low)], axis=1).astype(BF)
    got = swap(sent, "mp", 1).astype(F32)
    mine = block(part, 2 * high + low) + block(got, high)
    other = block(part, 2 * (1 - high) + low) + block(got, 1 - high)
    return mine + swap(other.astype(BF), "mp", 2).astype(F32)


def softmax_rows(query, keys, key_mask):
    scores = jnp.einsum("bqd,brd->bqr", query, keys, preferred_element_type=F32) * HD ** (-0.5)
    scores = jnp.where(key_mask[:, None, :], scores, -1e30)
    raised = jnp.exp(scores - jnp.max(scores, axis=-1, keepdims=True))
    return raised / jnp.sum(raised, axis=-1, keepdims=True)


def attend_back(query, mixed_cot, keys, values, key_mask):
    probs = softmax_rows(query, keys, key_mask)
    prob_cot = jnp.einsum("bqd,brd->bqr", mixed_cot, values, preferred_element_type=F32)
    score_cot = (
        probs * (prob_cot - jnp.sum(prob_cot * probs, axis=-1, keepdims=True)) * HD ** (-0.5)
    ).astype(BF)
    query_cot = jnp.einsum("bqr,brd->bqd", score_cot, keys, preferred_element_type=F32).astype(BF)
    key_cot = jnp.einsum("bqr,bqd->brd", score_cot, query, preferred_element_type=F32)
    value_cot = jnp.einsum("bqr,bqd->brd", probs.astype(BF), mixed_cot, preferred_element_type=F32)
    return query_cot, jnp.concatenate([key_cot, value_cot], axis=-1).astype(BF)


def times_transposed(value, weight):
    return lax.dot_general(value, weight, (((1,), (1,)), ((), ())), preferred_element_type=F32)


def local(
    images,
    ln_gain,
    projector,
    tile_counts,
    assign,
    text,
    text_start,
    w_query,
    w_key,
    w_value,
    w_out,
    gates,
    grad_out,
):
    segments = lax.axis_size("segment")
    groups = lax.axis_size("dp")
    members = lax.axis_size("mp")
    segment_id = lax.axis_index("segment")
    group_id = lax.axis_index("dp")
    member_id = lax.axis_index("mp")
    micro, length, feat_width = text.shape
    rows_img, proj_in = images.shape[1:]
    last_width = ln_gain.shape[0]
    query_width = w_query.shape[2]
    share = rows_img // members
    tokens = micro * length
    first = segment_id == 0
    gate_value = jnp.tanh(gates[0])
    query_weight, out_weight = w_query[0], w_out[0]
    key_weight, value_weight = w_key[0], w_value[0]
    kv_width = key_weight.shape[1]

    own_rows = lax.dynamic_slice_in_dim(images[0], member_id * share, share, 0)
    last_cols = own_rows[:, :last_width].astype(F32)
    center = last_cols - jnp.mean(last_cols, axis=-1, keepdims=True)
    inv_std = lax.rsqrt(jnp.mean(center * center, axis=-1, keepdims=True) + 1e-05)
    normed = center * inv_std
    tile_rows = jnp.concatenate([(normed * ln_gain).astype(BF), own_rows[:, last_width:]], axis=1)

    table = lax.all_gather(
        jnp.concatenate([assign, tile_counts])[None], ("segment", "dp"), axis=0, tiled=True
    ).reshape(segments, groups, 2)
    assigned, tiles = table[:, :, 0], table[:, :, 1]
    here = assigned // micro == group_id
    source = jnp.argmax(here, axis=1).astype(jnp.int32)
    slot_of = jnp.sum(jnp.where(here, assigned % micro, 0), axis=1)
    tiles_of = jnp.sum(jnp.where(here, tiles, 0), axis=1)
    seq_ids = jnp.arange(micro, dtype=jnp.int32)
    chosen = slot_of[None, :] == seq_ids[:, None]
    image_seg = jnp.argmax(chosen, axis=1).astype(jnp.int32)
    counts = jnp.sum(jnp.where(chosen, tiles_of[None, :], 0), axis=1)
    key_mask = jnp.arange(rows_img, dtype=jnp.int32)[None, :] < counts[:, None] * PATCH
    text_live = (
        jnp.arange(length, dtype=jnp.int32)[None, :] >= text_start[:, None]
    ).astype(F32)
    scale = (gate_value * text_live).reshape(tokens, 1)

    column = lax.all_gather(tile_rows, "dp", axis=0, tiled=False)
    mine = pick(column, pick(source, segment_id))
    tile_in = lax.all_gather(mine, ("segment", "mp"), axis=0, tiled=True)

    text_rows = text.reshape(tokens, feat_width)
    grad_rows = grad_out.reshape(tokens, feat_width)
    out_cot = (scale * grad_rows.astype(F32)).astype(BF)
    early = lax.cond(
        first,
        lambda: jnp.dot(text_rows, query_weight, preferred_element_type=F32),
        lambda: times_transposed(out_cot, out_weight),
    )
    early_sum = scatter_columns(early).astype(BF)

    def heads(array):
        return array.reshape(micro, -1, HD)

    def flat(array):
        return array.reshape(tokens, -1)

    features = jnp.dot(tile_in, projector, preferred_element_type=F32).astype(BF)
    key_part = jnp.dot(features, key_weight, preferred_element_type=F32)
    value_part = jnp.dot(features, value_weight, preferred_element_type=F32)
    per = kv_width // members
    parts = jnp.stack([key_part, value_part]).reshape(2, -1, members, per).transpose(2, 0, 1, 3)
    kv_image = scatter_sum(parts).astype(BF).reshape(2, segments, rows_img, per)
    kv = jnp.stack([pick(kv_image, image_seg[i], 1) for i in range(micro)], axis=1)
    keys, values = kv[0], kv[1]

    probs = softmax_rows(heads(early_sum), keys, key_mask)
    mixed = jnp.einsum("bqr,brd->bqd", probs.astype(BF), values, preferred_element_type=F32)
    mixed_all = lax.all_gather(flat(mixed.astype(BF)), "mp", axis=1, tiled=True)
    projected = jnp.dot(mixed_all, out_weight, preferred_element_type=F32)
    hidden = (text_rows.astype(F32) + scale * projected).astype(BF)
    hidden = swap(hidden, "segment", 1)

    query_late = scatter_columns(
        jnp.dot(hidden, query_weight, preferred_element_type=F32)
    ).astype(BF)
    query_cot, kv_cot_late = attend_back(
        heads(query_late), heads(early_sum), keys, values, key_mask
    )
    query_back = times_transposed(
        lax.all_gather(flat(query_cot), "mp", axis=1, tiled=True), query_weight
    )
    cot_late = (grad_rows.astype(F32) + query_back).astype(BF)
    cot_in = swap(cot_late, "segment", 1)

    out_cot = (scale * cot_in.astype(F32)).astype(BF)
    mixed_cot = scatter_columns(times_transposed(out_cot, out_weight)).astype(BF)
    query_cot, kv_cot_early = attend_back(
        heads(early_sum), heads(mixed_cot), keys, values, key_mask
    )
    kv_cot = jnp.where(first, kv_cot_early, kv_cot_late)
    kv_cot = jnp.stack([pick(kv_cot, slot_of[i]) for i in range(segments)])
    kv_all = lax.all_gather(kv_cot.reshape(segments * rows_img, 2 * per), "mp", axis=0)
    query_back = times_transposed(
        lax.all_gather(flat(query_cot), "mp", axis=1, tiled=True), query_weight
    )
    cot_early = (cot_in.astype(F32) + query_back).astype(BF)
    grads = jnp.where(first, cot_early, cot_late)

    key_all = kv_all[:, :, :per].transpose(1, 0, 2).reshape(-1, kv_width)
    value_all = kv_all[:, :, per:].transpose(1, 0, 2).reshape(-1, kv_width)
    feature_cot = (
        times_transposed(key_all, key_weight) + times_transposed(value_all, value_weight)
    ).astype(BF)
    norm_part = times_transposed(feature_cot, projector)
    parts = norm_part.reshape(segments, members, share, proj_in).transpose(1, 0, 2, 3)
    summed = scatter_sum(parts)
    returned = pick(summed, segment_id) + swap(
        pick(summed, 1 - segment_id).astype(BF), "segment", 1
    ).astype(F32)
    column = lax.all_gather(returned.astype(BF), "dp", axis=0, tiled=False)
    norm_cot = pick(column, assign[0] // micro).astype(F32)
    scaled = norm_cot[:, :last_width] * ln_gain
    last_grad = inv_std * (
        scaled
        - jnp.mean(scaled, axis=-1, keepdims=True)
        - normed * jnp.mean(scaled * normed, axis=-1, keepdims=True)
    )
    result = jnp.concatenate([last_grad, norm_cot[:, last_width:]], axis=1).astype(BF)
    result = lax.all_gather(result, "mp", axis=0, tiled=True)
    return (grads.reshape(1, micro, length, feat_width), result[None])


def solution(mesh):
    return jax.shard_map(
        local,
        mesh=mesh,
        in_specs=(
            P(("segment", "dp"), None, None),
            P(),
            P(None, "mp"),
            P(("segment", "dp")),
            P(("segment", "dp")),
            P("dp", None, "mp"),
            P("dp"),
            P("segment", "mp", None),
            P("segment", "mp", None),
            P("segment", "mp", None),
            P("segment", None, "mp"),
            P("segment"),
            P("dp", None, "mp"),
        ),
        out_specs=(P("segment", "dp", None, "mp"), P(("segment", "dp"), None, None)),
        check_vma=False,
    )
```

time: 599 us -> 357 us (0.60)
  waiting for transfers between devices: 225 us -> 99.4 us
  matrix products: 172 us -> 103 us
  blocking collectives: 95.5 us -> 69.8 us
  starting transfers between devices: 32.3 us -> 9.97 us
  between operations: 17.3 us -> 26.6 us
  local copies, waits for them, and re-layouts: 33.8 us -> 25.7 us
    reduce_scatter x7 -> x0, waiting for transfers between devices: 127 us -> none  [the longest x3 54.1 us: local(): lax.psum_scatter(query_part.astype(jnp.bfloat16), 'mp', scatter_dimension...]
    dot_general x40 -> x20, matrix products: 172 us -> 101 us  [the longest x5 51 us: times_transposed(): lax.dot_general(value, weight, (((1,), (1,)), ((), ())), preferred_elemen...]
    all_to_all x3 -> x0, blocking collectives: 44 us -> none  [the longest x1 19.1 us: local(): lax.all_to_all(back_pieces, 'dp', split_axis=0, concat_axis=0, tiled=True)]
    all_gather x1 -> x4, waiting for transfers between devices: 0.01 us -> 41.2 us  [the longest x2 21.8 us: local(): lax.all_gather(flat(query_cot), 'mp', axis=1, tiled=True)]
    ppermute x4 -> x13, waiting for transfers between devices: 25.5 us -> 58.1 us  [swap(): return lax.ppermute(value, axis, [(i, i ^ bit) for i in range(count)])]
    all_to_all x5 -> x0, waiting for transfers between devices: 26 us -> none  [the longest x1 13.7 us: local(): lax.all_to_all(pieces, 'dp', split_axis=0, concat_axis=0, tiled=True)]
    unnamed x13 -> x4, waiting for transfers between devices: 24.7 us -> 0.07 us
    psum x1 -> x0, waiting for transfers between devices: 21.9 us -> none  [local(): lax.psum(norm_part.astype(jnp.bfloat16), 'mp').astype(jnp.float32)]
  transfers between devices with their start and end apart: 20 -> 17, of which waited for: 18 -> 13; matrix products, arithmetic and copies ran while one was open for 14% -> 16% of each run, Pallas kernels for 0% -> 0%
where the time goes in v1:
time: 357 us; the launch traced here: 350 us
  matrix products  103 us (29%)
  waiting for transfers between devices  99.4 us (28%)
  blocking collectives  69.8 us (20%)
  between operations  26.6 us (7%)
  local copies, waits for them, and re-layouts  25.7 us (7%)
  other arithmetic  15.2 us (4%)
  starting transfers between devices  9.97 us (3%)
    ppermute x13, waiting for transfers between devices, swap(): return lax.ppermute(value, axis, [(i, i ^ bit) for i in range(count)])  58.1 us
    dot_general x5, matrix products, times_transposed(): lax.dot_general(value, weight, (((1,), (1,)), ((), ())), preferred_elemen...  51 us
    all_gather x2, waiting for transfers between devices, local(): lax.all_gather(flat(query_cot), 'mp', axis=1, tiled=True)  21.8 us
    all_gather x1, blocking collectives, local(): column = lax.all_gather(returned.astype(BF), 'dp', axis=0, tiled=False)  21.7 us
    all_gather x1, blocking collectives, local(): column = lax.all_gather(tile_rows, 'dp', axis=0, tiled=False)  19.4 us
    all_gather x1, waiting for transfers between devices, local(): mixed_all = lax.all_gather(flat(mixed.astype(BF)), 'mp', axis=1, tiled=True)  16.7 us
    unnamed x1, blocking collectives  13 us
    dot_general x1, matrix products, local(): jnp.dot(tile_in, projector, preferred_element_type=F32).astype(BF)  10.4 us
  transfers between devices with their start and end apart: 17, of which 13 were waited for; matrix products, arithmetic and copies ran while one was open for 16% of the time, Pallas kernels for 0%

profile of v1, /device:TPU:0, one launch (start us, length us, event | category | flops | bytes accessed | tf_op | source)
XLA Modules:
  0.0 350.3 jit_solution(7315036304372386585)
XLA Ops:
  7.3 1.1 copy-done
  9.9 1.2 dynamic-slice.1
  12.0 13.0 %all-reduce = s32[16]{0:T(128)S(1)} all-reduce(s32[16]{0:T(128)S(1)} %add_dynamic-update-slice_fusion), channel_id=2, replica_groups=mesh['segment'=2,'dp'=4,'mp'=4] {'segment','dp'}, use_global_device_ids=true, to_apply=%add | all-reduce | flops 16 | bytes 128
  29.0 19.4 %all-gather.1 = bf16[128,3840]{1,0:T(8,128)(2,1)S(1)} all-gather(bf16[32,3840]{1,0:T(8,128)(2,1)S(1)} %pad_maximum_fusion.4), channel_id=3, replica_groups=mesh['segment'=2,'dp'=4,'mp'=4] {'dp'}, dimensions={0}, use_global_device_ids=true | all-gather | bytes 1228800 | tf_op jit(solution)/shard_map/all_gather | solution.py:127
  50.7 0.9 fusion.30
  51.7 8.9 %conditional.1 = (f32[128,4096]{1,0:T(8,128)S(1)}) conditional(s32[]{:T(128)} %convert_element_type.167, (bf16[128,2048]{1,0:T(8,128)(2,1)}, bf16[4096,2048]{1,0:T(8,128)(2,1)}) %tuple.49, (bf16[128,2048]{1,0:T(8,128)(2,1)S(1)}, bf16[2048,4096]{1,0:T(8,128)(2,1)}) %tuple.50), branch_computations={%region_3.4_spmd, %region_4.5_spmd} | conditional | flops 2147483648 | bytes 19398664 | solution.py:134
  51.7 8.4 %fusion.109 = f32[128,4096]{1,0:T(8,128)S(1)} fusion(bf16[128,2048]{1,0:T(8,128)(2,1)S(1)} %get-tuple-element.13, bf16[2048,4096]{1,0:T(8,128)(2,1)} %get-tuple-element.14), kind=kOutput, calls=%fused_computation.185 | convolution fusion | flops 2147483648 | bytes 19398656 | tf_op jit(solution)/shard_map/cond/branch_1_fun/dot_general | solution.py:136
  60.7 0.9 pad_maximum_fusion.1
  65.2 4.1 %copy.88 = bf16[512,2048]{1,0:T(8,128)(2,1)} copy(bf16[512,2048]{0,1:T(8,128)(2,1)} %bitcast.151) | data formatting | bytes 4194304 | tf_op jit(solution)/shard_map/dot_general | solution.py:149
  69.3 2.5 copy.87
  73.1 2.8 all-gather.15.cloned.1.call-done
  75.9 10.4 %fusion.5 = bf16[256,2048,1]{1,0,2:T(8,128)(2,1)S(1)} fusion(bf16[3840,2048]{1,0:T(8,128)(2,1)} %param.17, bf16[1,256,3840]{2,1,0:T(8,128)(2,1)} %all-gather.15.cloned.1.call-done), kind=kOutput, calls=%fused_computation.7 | convolution fusion | flops 4027056128 | bytes 18743296 | tf_op jit(solution)/shard_map/dot_general | solution.py:147
  87.1 0.8 copy-done.9
  89.2 1.2 convert_element_type.169
  90.6 1.5 collective-permute-start.1
  93.6 6.2 %collective-permute-done.1 = bf16[128,1024]{1,0:T(8,128)(2,1)S(1)} collective-permute-done((bf16[128,1024]{1,0:T(8,128)(2,1)S(1)}, bf16[128,1024]{1,0:T(8,128)(2,1)S(1)}, u32[]{:S(2)}, u32[]{:S(2)}) %collective-permute-start.1) | collective-permute-done | bytes 262176 | tf_op jit(solution)/shard_map/ppermute | solution.py:14
  100.6 1.1 reshape.150
  101.9 1.0 fusion.49
  102.9 1.1 fusion.106
  104.1 1.2 convolution_convert_fusion.3
  105.3 1.8 reshape.153
  107.3 16.7 %all-gather.9.cloned.1.call-done = bf16[128,4096]{1,0:T(8,128)(2,1)} async-done(((bf16[128,1024]{1,0:T(8,128)(2,1)}), bf16[128,4096]{1,0:T(8,128)(2,1)}) %all-gather.9.cloned.1.call-update) | async-done | bytes 1048592 | tf_op jit(solution)/shard_map/all_gather | solution.py:158
  124.0 8.5 %fusion.9 = bf16[128,2048]{1,0:T(8,128)(2,1)S(1)} fusion(bf16[128,4096]{1,0:T(8,128)(2,1)} %all-gather.9.cloned.1.call-done, bf16[128,2048]{1,0:T(8,128)(2,1)S(1)} %bitcast.147, f32[128]{0:T(128)S(1)} %mul.149, bf16[1,4096,2048]{2,1,0:T(8,128)(2,1)} %param.25), kind=kOutput, calls=%fused_computation.14 | convolution fusion | flops 2148532224 | bytes 18874880 | tf_op jit(solution)/shard_map/dot_general | solution.py:159
  132.5 1.5 collective-permute-start.4
  134.0 12.6 %collective-permute-done.4 = bf16[128,2048]{1,0:T(8,128)(2,1)S(1)} collective-permute-done((bf16[128,2048]{1,0:T(8,128)(2,1)S(1)}, bf16[128,2048]{1,0:T(8,128)(2,1)S(1)}, u32[]{:S(2)}, u32[]{:S(2)}) %collective-permute-start.4) | collective-permute-done | bytes 524320 | tf_op jit(solution)/shard_map/ppermute | solution.py:14
  146.6 8.1 %fusion.83 = f32[128,4096]{1,0:T(8,128)S(1)} fusion(bf16[128,2048]{1,0:T(8,128)(2,1)S(1)} %collective-permute-done.4, bf16[1,2048,4096]{2,1,0:T(8,128)(2,1)} %param.22), kind=kOutput, calls=%fused_computation.163 | convolution fusion | flops 2147483648 | bytes 19398656 | tf_op jit(solution)/shard_map/dot_general | solution.py:164
  154.9 1.9 collective-permute-done.5
  157.4 1.0 fusion.99
  158.4 7.0 %collective-permute-done.6 = bf16[128,1024]{1,0:T(8,128)(2,1)S(1)} collective-permute-done((bf16[128,1024]{1,0:T(8,128)(2,1)S(1)}, bf16[128,1024]{1,0:T(8,128)(2,1)S(1)}, u32[]{:S(2)}, u32[]{:S(2)}) %collective-permute-start.6) | collective-permute-done | bytes 262176 | tf_op jit(solution)/shard_map/ppermute | solution.py:14
  165.7 1.1 fusion.107
  166.8 2.2 convolution_convert_fusion.2
  169.0 0.8 reshape.155
  170.1 16.6 %all-gather.11.cloned.1.call-done = bf16[128,4096]{1,0:T(8,128)(2,1)} async-done(((bf16[128,1024]{1,0:T(8,128)(2,1)}), bf16[128,4096]{1,0:T(8,128)(2,1)}) %all-gather.11.cloned.1.call-update) | async-done | bytes 1048592 | tf_op jit(solution)/shard_map/all_gather | solution.py:170
  186.7 11.8 %fusion.7 = bf16[128,2048]{1,0:T(8,128)(2,1)S(1)} fusion(bf16[128,4096]{1,0:T(8,128)(2,1)} %all-gather.11.cloned.1.call-done, bf16[128,2048]{1,0:T(8,128)(2,1)} %bitcast.150, bf16[1,2048,4096]{2,1,0:T(8,128)(2,1)} %param.22), kind=kOutput, calls=%fused_computation.12 | convolution fusion | flops 2148270080 | bytes 18874368 | tf_op jit(solution)/shard_map/dot_general | solution.py:66
  198.5 1.5 collective-permute-start.7
  200.1 12.7 %collective-permute-done.7 = bf16[128,2048]{1,0:T(8,128)(2,1)} collective-permute-done((bf16[128,2048]{1,0:T(8,128)(2,1)S(1)}, bf16[128,2048]{1,0:T(8,128)(2,1)}, u32[]{:S(2)}, u32[]{:S(2)}) %collective-permute-start.7) | collective-permute-done | bytes 524320 | tf_op jit(solution)/shard_map/ppermute | solution.py:14
  212.8 13.0 %fusion.43 = f32[128,4096]{1,0:T(8,128)} fusion(bf16[128,2048]{1,0:T(8,128)(2,1)} %collective-permute-done.7, f32[128]{0:T(128)S(1)} %mul.149, bf16[1,4096,2048]{2,1,0:T(8,128)(2,1)} %param.25), kind=kOutput, calls=%fused_computation.62 | convolution fusion | flops 2148270080 | bytes 19399168 | tf_op jit(solution)/shard_map/dot_general | solution.py:66
  225.8 1.3 dynamic-slice_convert_fusion.3
  227.0 0.8 pad_maximum_fusion.3
  232.4 1.0 copy-done.5
  233.4 1.2 add_convert_fusion.1
  234.9 2.2 convolution_convert_fusion.5
  237.7 5.8 %collective-permute-done.9 = bf16[128,1024]{1,0:T(8,128)(2,1)} collective-permute-done((bf16[128,1024]{1,0:T(8,128)(2,1)S(1)}, bf16[128,1024]{1,0:T(8,128)(2,1)}, u32[]{:S(2)}, u32[]{:S(2)}) %collective-permute-start.9) | collective-permute-done | bytes 262176 | tf_op jit(solution)/shard_map/ppermute | solution.py:14
  243.4 1.4 add_convert_fusion
  245.4 1.0 fusion.97
  246.5 2.2 convolution_convert_fusion.7
  248.9 6.9 %all_gather.40 = bf16[4,256,256]{2,1,0:T(8,128)(2,1)S(1)} all-gather(bf16[1,256,256]{2,1,0:T(8,128)(2,1)S(1)} %bitcast.159), channel_id=1, replica_groups=mesh['segment'=2,'dp'=4,'mp'=4] {'mp'}, dimensions={0}, use_global_device_ids=true | all-gather | bytes 655360 | tf_op jit(solution)/shard_map/all_gather | solution.py:182
  256.6 1.1 copy.90
  257.9 2.1 fusion.12
  260.0 11.6 %fusion.32 = f32[256,3840]{1,0:T(8,128)} fusion(bf16[3840,2048]{1,0:T(8,128)(2,1)} %param.17, f32[256,2048]{1,0:T(8,128)} %fusion.12, bf16[256,512]{0,1:T(8,128)(2,1)S(1)} %bitcast.160, bf16[1,2048,512]{2,1,0:T(8,128)(2,1)} %param.24), kind=kOutput, calls=%fused_computation.52 | convolution fusion | flops 4564451328 | bytes 24117248 | tf_op jit(solution)/shard_map/dot_general | solution.py:66
  271.6 1.6 fusion.42
  273.6 2.2 collective-permute-done.10
  275.8 1.7 bitcast_add_fusion
  277.6 1.1 collective-permute-start.11
  278.7 2.2 convolution_convert_fusion.1
  281.0 0.8 reshape.157
  281.8 9.4 %collective-permute-done.11 = bf16[2,32,3840]{2,1,0:T(8,128)(2,1)} collective-permute-done((bf16[2,32,3840]{2,1,0:T(8,128)(2,1)S(1)}, bf16[2,32,3840]{2,1,0:T(8,128)(2,1)}, u32[]{:S(2)}, u32[]{:S(2)}) %collective-permute-start.11) | collective-permute-done | bytes 491552 | tf_op jit(solution)/shard_map/ppermute | solution.py:14
  291.3 1.1 bitcast_add_fusion.1
  292.4 1.5 collective-permute-start.12
  293.9 5.2 %all-gather.13.cloned.1.call-done = bf16[128,4096]{1,0:T(8,128)(2,1)} async-done(((bf16[128,1024]{1,0:T(8,128)(2,1)}), bf16[128,4096]{1,0:T(8,128)(2,1)}) %all-gather.13.cloned.1.call-update) | async-done | bytes 1048592 | tf_op jit(solution)/shard_map/all_gather | solution.py:184
  299.1 12.6 %fusion.10 = bf16[128,2048]{1,0:T(8,128)(2,1)} fusion(bf16[128,2048]{1,0:T(8,128)(2,1)} %copy-done.7, bf16[128,4096]{1,0:T(8,128)(2,1)} %all-gather.13.cloned.1.call-done, bf16[128,2048]{1,0:T(8,128)(2,1)} %collective-permute-done.7, pred[]{:T(512)S(6)} %eq.34, bf16[1,2048,4096]{2,1,0:T(8,128)(2,1)} %param.22), kind=kOutput, calls=%fused_computation.15 | convolution fusion | flops 2148532224 | bytes 19398656 | tf_op jit(solution)/shard_map/dot_general | solution.py:66
  311.7 21.7 %all-gather.3 = bf16[128,3840]{1,0:T(8,128)(2,1)S(1)} all-gather(bf16[32,3840]{1,0:T(8,128)(2,1)S(1)} %fusion.47), channel_id=5, replica_groups=mesh['segment'=2,'dp'=4,'mp'=4] {'dp'}, dimensions={0}, use_global_device_ids=true | all-gather | bytes 1228800 | tf_op jit(solution)/shard_map/all_gather | solution.py:200
  333.9 8.7 %all_gather.43 = bf16[128,3840]{1,0:T(8,128)(2,1)S(1)} all-gather(bf16[32,3840]{1,0:T(8,128)(2,1)S(1)} %pad_maximum_fusion.5), channel_id=1, replica_groups=mesh['segment'=2,'dp'=4,'mp'=4] {'mp'}, dimensions={0}, use_global_device_ids=true | all-gather | bytes 1228800 | tf_op jit(solution)/shard_map/all_gather | solution.py:209
  342.6 0.9 copy.98
  (110 shorter events, 16.0 us)
Async XLA Ops:
  7.2 1.2 copy-start
  7.2 43.4 %copy-start.15 = (s32[2]{0:T(128)S(1)}, s32[2]{0:T(128)}, u32[]{:S(2)}) copy-start(s32[2]{0:T(128)} %param.21) | copy-start | bytes 28
  7.2 43.5 %copy-start.8 = (bf16[2,64,2048]{2,1,0:T(8,128)(2,1)S(1)}, bf16[2,64,2048]{2,1,0:T(8,128)(2,1)}, u32[]{:S(2)}) copy-start(bf16[2,64,2048]{2,1,0:T(8,128)(2,1)} %param.27) | copy-start | bytes 1572868
  7.2 68.7 %all-gather.15.cloned.1.call-start = ((), (), s32[]{:S(2)}) async-start(), calls=%async_computation.3 | async-start | bytes 2211840 | tf_op jit(solution)/shard_map/all_gather | solution.py:129
  8.5 43.1 %copy-start.6 = (bf16[2,64,2048]{2,1,0:T(8,128)(2,1)S(1)}, bf16[2,64,2048]{2,1,0:T(8,128)(2,1)}, u32[]{:S(2)}) copy-start(bf16[2,64,2048]{2,1,0:T(8,128)(2,1)} %param.20) | copy-start | bytes 1572868
  49.8 74.2 %all-gather.9.cloned.1.call-start = ((), (), s32[]{:S(2)}) async-start(), calls=%async_computation | async-start | bytes 1310720 | tf_op jit(solution)/shard_map/all_gather | solution.py:158
  60.6 4.6 %copy-start.3 = (f32[128,4096]{1,0:T(8,128)}, f32[128,4096]{1,0:T(8,128)S(1)}, u32[]{:S(2)}) copy-start(f32[128,4096]{1,0:T(8,128)S(1)} %get-tuple-element.54) | copy-start | bytes 6291460
  61.6 27.6 %collective-permute-start = (bf16[128,2048]{1,0:T(8,128)(2,1)}, bf16[128,2048]{1,0:T(8,128)(2,1)}, u32[]{:S(2)}, u32[]{:S(2)}) collective-permute-start(bf16[128,2048]{1,0:T(8,128)(2,1)} %pad_maximum_fusion.1), channel_id=1, source_target_pairs={{0,1},{1,0},{2,3},{3,2},{4,5},{5,4},{6,7},{7,6},{8,9},{9,8},{10,11... | collective-permute-start | bytes 1572872 | tf_op jit(solution)/shard_map/ppermute | solution.py:14
  65.2 4.1 %copy-start.2 = (bf16[1,2048,512]{2,1,0:T(8,128)(2,1)S(1)}, bf16[1,2048,512]{2,1,0:T(8,128)(2,1)}, u32[]{:S(2)}) copy-start(bf16[1,2048,512]{2,1,0:T(8,128)(2,1)} %param.23) | copy-start | bytes 6291460
  75.9 10.4 %copy-start.10 = (bf16[512,2048]{1,0:T(8,128)(2,1)S(1)}, bf16[512,2048]{1,0:T(8,128)(2,1)}, u32[]{:S(2)}) copy-start(bf16[512,2048]{1,0:T(8,128)(2,1)} %copy.88) | copy-start | bytes 6291460
  86.4 1.6 copy-start.9
  88.7 1.8 copy-start.4
  88.8 3.2 collective-permute-start.2
  90.6 9.2 %collective-permute-start.1 = (bf16[128,1024]{1,0:T(8,128)(2,1)S(1)}, bf16[128,1024]{1,0:T(8,128)(2,1)S(1)}, u32[]{:S(2)}, u32[]{:S(2)}) collective-permute-start(bf16[128,1024]{1,0:T(8,128)(2,1)S(1)} %add_convert_fusion.5), channel_id=1, source_target_pairs={{0,2},{1,3},{2,0},{3,1},{4,6},{5,7},{6,4},{7,5},{8,10},{9,11},{10,... | collective-permute-start | bytes 786440 | tf_op jit(solution)/shard_map/ppermute | solution.py:14
  92.1 0.8 copy-start.11
  92.9 9.0 %collective-permute-start.3 = (bf16[2,256,128]{2,1,0:T(8,128)(2,1)S(1)}, bf16[2,256,128]{2,1,0:T(8,128)(2,1)S(1)}, u32[]{:S(2)}, u32[]{:S(2)}) collective-permute-start(bf16[2,256,128]{2,1,0:T(8,128)(2,1)S(1)} %fusion.68), channel_id=1, source_target_pairs={{0,2},{1,3},{2,0},{3,1},{4,6},{5,7},{6,4},{7,5},{8,10},{9,11},{10,... | collective-permute-start | bytes 393224 | tf_op jit(solution)/shard_map/ppermute | solution.py:14
  107.1 79.6 %all-gather.11.cloned.1.call-start = ((), (), s32[]{:S(2)}) async-start(), calls=%async_computation.1 | async-start | bytes 1310720 | tf_op jit(solution)/shard_map/all_gather | solution.py:170
  132.5 14.1 %collective-permute-start.4 = (bf16[128,2048]{1,0:T(8,128)(2,1)S(1)}, bf16[128,2048]{1,0:T(8,128)(2,1)S(1)}, u32[]{:S(2)}, u32[]{:S(2)}) collective-permute-start(bf16[128,2048]{1,0:T(8,128)(2,1)S(1)} %fusion.9), channel_id=1, source_target_pairs={{0,16},{16,0},{1,17},{17,1},{2,18},{18,2},{3,19},{19,3},{4,20},{20... | collective-permute-start | bytes 1572872 | tf_op jit(solution)/shard_map/ppermute | solution.py:14
  154.9 2.0 collective-permute-start.5
  157.0 8.4 %collective-permute-start.6 = (bf16[128,1024]{1,0:T(8,128)(2,1)S(1)}, bf16[128,1024]{1,0:T(8,128)(2,1)S(1)}, u32[]{:S(2)}, u32[]{:S(2)}) collective-permute-start(bf16[128,1024]{1,0:T(8,128)(2,1)S(1)} %add_convert_fusion.3), channel_id=1, source_target_pairs={{0,2},{1,3},{2,0},{3,1},{4,6},{5,7},{6,4},{7,5},{8,10},{9,11},{10,... | collective-permute-start | bytes 786440 | tf_op jit(solution)/shard_map/ppermute | solution.py:14
  165.7 4.1 %copy-start.12 = (bf16[2,512,128]{2,1,0:T(8,128)(2,1)}, bf16[2,512,128]{2,1,0:T(8,128)(2,1)S(1)}, u32[]{:S(2)}) copy-start(bf16[2,512,128]{2,1,0:T(8,128)(2,1)S(1)} %reshape.154) | copy-start | bytes 786436
  169.9 129.2 %all-gather.13.cloned.1.call-start = ((), (), s32[]{:S(2)}) async-start(), calls=%async_computation.2 | async-start | bytes 1310720 | tf_op jit(solution)/shard_map/all_gather | solution.py:184
  198.5 27.2 %copy-start.7 = (bf16[128,2048]{1,0:T(8,128)(2,1)}, bf16[128,2048]{1,0:T(8,128)(2,1)S(1)}, u32[]{:S(2)}) copy-start(bf16[128,2048]{1,0:T(8,128)(2,1)S(1)} %fusion.7) | copy-start | bytes 1572868
  198.5 14.2 %collective-permute-start.7 = (bf16[128,2048]{1,0:T(8,128)(2,1)S(1)}, bf16[128,2048]{1,0:T(8,128)(2,1)}, u32[]{:S(2)}, u32[]{:S(2)}) collective-permute-start(bf16[128,2048]{1,0:T(8,128)(2,1)S(1)} %fusion.7), channel_id=1, source_target_pairs={{0,16},{16,0},{1,17},{17,1},{2,18},{18,2},{3,19},{19,3},{4,20},{20... | collective-permute-start | bytes 1572872 | tf_op jit(solution)/shard_map/ppermute | solution.py:14
  227.9 4.4 %collective-permute-start.8 = (bf16[128,2048]{1,0:T(8,128)(2,1)}, bf16[128,2048]{1,0:T(8,128)(2,1)S(1)}, u32[]{:S(2)}, u32[]{:S(2)}) collective-permute-start(bf16[128,2048]{1,0:T(8,128)(2,1)} %pad_maximum_fusion.3), channel_id=1, source_target_pairs={{0,1},{1,0},{2,3},{3,2},{4,5},{5,4},{6,7},{7,6},{8,9},{9,8},{10,11... | collective-permute-start | bytes 1572872 | tf_op jit(solution)/shard_map/ppermute | solution.py:14
  232.4 1.0 copy-start.5
  233.4 3.8 %copy-start.13 = (bf16[2,512,128]{2,1,0:T(8,128)(2,1)S(1)}, bf16[2,512,128]{2,1,0:T(8,128)(2,1)}, u32[]{:S(2)}) copy-start(bf16[2,512,128]{2,1,0:T(8,128)(2,1)} %copy-done.12) | copy-start | bytes 786436
  234.5 8.9 %collective-permute-start.9 = (bf16[128,1024]{1,0:T(8,128)(2,1)S(1)}, bf16[128,1024]{1,0:T(8,128)(2,1)}, u32[]{:S(2)}, u32[]{:S(2)}) collective-permute-start(bf16[128,1024]{1,0:T(8,128)(2,1)S(1)} %add_convert_fusion.1), channel_id=1, source_target_pairs={{0,2},{1,3},{2,0},{3,1},{4,6},{5,7},{6,4},{7,5},{8,10},{9,11},{10,... | collective-permute-start | bytes 786440 | tf_op jit(solution)/shard_map/ppermute | solution.py:14
  273.2 2.6 collective-permute-start.10
  277.6 13.6 %collective-permute-start.11 = (bf16[2,32,3840]{2,1,0:T(8,128)(2,1)S(1)}, bf16[2,32,3840]{2,1,0:T(8,128)(2,1)}, u32[]{:S(2)}, u32[]{:S(2)}) collective-permute-start(bf16[2,32,3840]{2,1,0:T(8,128)(2,1)S(1)} %fusion.46), channel_id=1, source_target_pairs={{0,2},{1,3},{2,0},{3,1},{4,6},{5,7},{6,4},{7,5},{8,10},{9,11},{10,... | collective-permute-start | bytes 1474568 | tf_op jit(solution)/shard_map/ppermute | solution.py:14
  292.4 19.2 %collective-permute-start.12 = (bf16[32,3840]{1,0:T(8,128)(2,1)S(1)}, bf16[32,3840]{1,0:T(8,128)(2,1)S(1)}, u32[]{:S(2)}, u32[]{:S(2)}) collective-permute-start(bf16[32,3840]{1,0:T(8,128)(2,1)S(1)} %fusion.55), channel_id=1, source_target_pairs={{0,16},{16,0},{1,17},{17,1},{2,18},{18,2},{3,19},{19,3},{4,20},{20... | collective-permute-start | bytes 737288 | tf_op jit(solution)/shard_map/ppermute | solution.py:14
  311.7 21.8 %copy-start.14 = (f32[1280]{0:T(1024)S(1)}, f32[1280]{0:T(1024)}, u32[]{:S(2)}) copy-start(f32[1280]{0:T(1024)} %param.16) | copy-start | bytes 15364
  333.5 10.1 %copy-start.1 = (bf16[1,128,3840]{2,1,0:T(8,128)(2,1)S(1)}, bf16[1,128,3840]{2,1,0:T(8,128)(2,1)}, u32[]{:S(2)}) copy-start(bf16[1,128,3840]{2,1,0:T(8,128)(2,1)} %param.15) | copy-start | bytes 2949124
Sparse Core Ops, SparseCore 0:
  49.9 25.9 all-gather.14
  107.2 16.7 all-gather.8
  170.0 16.7 all-gather.10
  281.9 17.1 all-gather.12
